TPU v7x, 1024 devices: a whole 8x8x8 slice. The times are simulated.
1024 devices in a mesh: tm: 64 (over x, y_lo, core), row: 2 (over y_hi), col: 8 (over z).
Axes of the slice: x: 8, y: 8 (y_hi: 2, y_lo: 4; y = y_hi * 4 + y_lo), z: 8, core: 2. Of those that a mesh axis runs over, the one named last changes fastest.
Arguments:
- query: bfloat16 [64, 16, 128, 1024], P('tm', 'row', 'col'), may hold values from -6 to 6
- key: bfloat16 [64, 16, 128, 1024], P('tm', 'row', 'col'), may hold values from -6 to 6
- value: bfloat16 [64, 16, 128, 1024], P('tm', 'row', 'col'), may hold values from -6 to 6
- out_grad: bfloat16 [64, 16, 128, 1024], P('tm', 'row', 'col'), may hold values from -6 to 6
- tile_window: int32 [64, 2, 9], replicated, may hold values 0 or 1
- period_link: int32 [64], replicated, may hold values from 0 to 1, as said below
Outputs:
- attn_out: bfloat16 [64, 16, 128, 1024], P('tm', 'row', 'col')
- query_grad: bfloat16 [64, 16, 128, 1024], P('tm', 'row', 'col')
- key_grad: bfloat16 [64, 16, 128, 1024], P('tm', 'row', 'col')
- value_grad: bfloat16 [64, 16, 128, 1024], P('tm', 'row', 'col')
Inputs may be any that keep to these rules, and one draw needn't show every extreme that they name: `period_link`: among periods 1 to 63 at least one has link 0 and at least one has link 1.
All inputs are finite; a program needn't handle non-finite values.
Results may differ from a plain program's by a relative error of at most 0.035.
Values may be sent and summed in bfloat16 or wider, within the bound.
A program may use at most 64 MiB of HBM per device.

v0:
```python
import functools
import math

import jax
import jax.numpy as jnp
from jax import lax
from jax.experimental import pallas as pl
from jax.experimental.pallas import tpu as pltpu
from jax.sharding import PartitionSpec as P

HD = 128
S = 4
ROWS = 8
COLS = 16
OWN = ROWS * COLS
HALF = S * COLS
EDGE = ROWS * S
CORNER = S * S
SIDE = EDGE + CORNER
AREA = OWN + HALF + 2 * SIDE
R_AT = OWN
L_AT = OWN + HALF
E_AT = L_AT + SIDE
NEG = -1e30
MESH = pl.DeviceIdType.MESH
F32 = jnp.float32
BF16 = jnp.bfloat16

COMPUTE = True
RELAY = True
UNROLL = 1


def nt(a, b):
    return lax.dot_general(a, b, (((1,), (1,)), ((), ())), preferred_element_type=F32)


def nn(a, b):
    return lax.dot_general(a, b, (((1,), (0,)), ((), ())), preferred_element_type=F32)


def edge_pick(rows):
    count = rows * S
    out = lax.broadcasted_iota(jnp.int32, (2 * count, rows * COLS), 0)
    src = lax.broadcasted_iota(jnp.int32, (2 * count, rows * COLS), 1)
    right = (out >= count).astype(jnp.int32)
    place = out - right * count
    want = lax.shift_right_logical(place, 2) * COLS + lax.bitwise_and(place, 3) + right * (COLS - S)
    return jnp.where(src == want, 1.0, 0.0).astype(BF16)


def kernel(
    window, link, q_ref, k_ref, v_ref, g_ref, o_ref, dq_ref, dk_ref, dv_ref,
    kv, qg, stats, relay, pack_own, pack_r, pack_t, pack_tr, spack, sown, bias_f, bias_b, stat_rows,
    send, recv, relay_send, relay_recv, ssend, srecv, *, heads, periods, n_cols,
):
    channels = heads * HD
    scale = 1.0 / math.sqrt(HD)
    p = lax.axis_index("tm")
    r = lax.axis_index("row")
    c = lax.axis_index("col")
    nxt = lax.rem(p + 1, periods)
    prv = lax.rem(p + periods - 1, periods)
    mate = 1 - r
    left = lax.rem(c + n_cols - 1, n_cols)
    right = lax.rem(c + 1, n_cols)
    y_lo = lax.rem(p // 2, 4)
    high = y_lo // 2
    far = p + 4 - 8 * high
    ahead = r + high - 2 * r * high
    behind = 1 - ahead

    barrier = pltpu.get_barrier_semaphore()
    friends = [
        (t, row, col)
        for t in (p, prv, nxt)
        for row in (r, mate)
        for col in (c, left, right)
        if not (t is p and row is r and col is c)
    ]
    if RELAY:
        friends += [(far, r, c), (far, mate, c)]
    for friend in friends:
        pl.semaphore_signal(barrier, inc=1, device_id=friend, device_id_type=MESH)

    kv[:OWN, :channels] = k_ref[...]
    kv[:OWN, channels:] = v_ref[...]
    qg[:OWN, :channels] = q_ref[...]
    qg[:OWN, channels:] = g_ref[...]
    half_at = pl.multiple_of(HALF * (1 - r), HALF)
    pl.semaphore_wait(barrier, len(friends))

    bufs = (kv, qg)
    toward = (nxt, prv)
    pending = []

    def copy(src, dst, a, b, i, device):
        return pltpu.make_async_remote_copy(
            src_ref=src, dst_ref=dst, send_sem=a.at[i], recv_sem=b.at[i],
            device_id=device, device_id_type=MESH,
        )

    def go(x, slot, src, at, size, device):
        op = copy(src, bufs[x].at[pl.ds(at, size)], send, recv, x * 11 + slot, device)
        op.start()
        pending.append(op)
        return op

    got = {}

    def begin(x):
        buf = bufs[x]
        t = toward[x]
        if RELAY:
            for way in range(2):
                op = copy(
                    buf.at[pl.ds(pl.multiple_of(half_at + way * (HALF // 2), HALF // 2), HALF // 2)],
                    relay.at[x, way], relay_send, relay_recv, x * 4 + way,
                    (far, ahead if way == 0 else behind, c),
                )
                op.start()
                pending.append(op)
                got[x, "hop", way] = op
        else:
            got[x, "r"] = go(x, 0, buf.at[pl.ds(half_at, HALF)], R_AT, HALF, (p, mate, c))
        got[x, "t"] = go(x, 1, buf.at[pl.ds(0, OWN)], AREA, OWN, (t, r, c))
        pack_own[x] = nn(edge_pick(ROWS), buf[:OWN, :]).astype(BF16)
        got[x, "le"] = go(x, 2, pack_own.at[x, pl.ds(0, EDGE)], E_AT, EDGE, (p, r, left))
        got[x, "re"] = go(x, 3, pack_own.at[x, pl.ds(EDGE, EDGE)], L_AT, EDGE, (p, r, right))

    def hop(x):
        if RELAY:
            for way in range(2):
                got[x, "hop", way].wait_recv()
                op = copy(
                    relay.at[x, way],
                    bufs[x].at[pl.ds(R_AT + way * (HALF // 2), HALF // 2)],
                    relay_send, relay_recv, x * 4 + 2 + way,
                    (far, ahead if way == 0 else behind, c),
                )
                op.start()
                pending.append(op)
                got[x, "r", way] = op

    def after_r(x):
        buf = bufs[x]
        if RELAY:
            for way in range(2):
                got[x, "r", way].wait_recv()
        else:
            got[x, "r"].wait_recv()
        got[x, "tr"] = go(x, 4, buf.at[pl.ds(R_AT, HALF)], AREA + R_AT, HALF, (toward[x], r, c))
        pack_r[x] = nn(edge_pick(S), buf[R_AT:L_AT, :]).astype(BF16)
        got[x, "lc"] = go(x, 5, pack_r.at[x, pl.ds(0, CORNER)], E_AT + EDGE, CORNER, (p, r, left))
        got[x, "rc"] = go(x, 6, pack_r.at[x, pl.ds(CORNER, CORNER)], L_AT + EDGE, CORNER, (p, r, right))

    def after_t(x):
        buf = bufs[x]
        got[x, "t"].wait_recv()
        pack_t[x] = nn(edge_pick(ROWS), buf[AREA:AREA + OWN, :]).astype(BF16)
        got[x, "tle"] = go(x, 7, pack_t.at[x, pl.ds(0, EDGE)], AREA + E_AT, EDGE, (p, r, left))
        got[x, "tre"] = go(x, 8, pack_t.at[x, pl.ds(EDGE, EDGE)], AREA + L_AT, EDGE, (p, r, right))

    def after_tr(x):
        buf = bufs[x]
        got[x, "tr"].wait_recv()
        pack_tr[x] = nn(edge_pick(S), buf[AREA + R_AT:AREA + L_AT, :]).astype(BF16)
        got[x, "tlc"] = go(x, 9, pack_tr.at[x, pl.ds(0, CORNER)], AREA + E_AT + EDGE, CORNER, (p, r, left))
        got[x, "trc"] = go(x, 10, pack_tr.at[x, pl.ds(CORNER, CORNER)], AREA + L_AT + EDGE, CORNER, (p, r, right))

    def finish(x):
        for name in ("le", "re", "lc", "rc", "tle", "tre", "tlc", "trc"):
            got[x, name].wait_recv()

    begin(0)
    begin(1)

    token = lax.broadcasted_iota(jnp.int32, (OWN, 1), 0)
    own_row = lax.shift_right_logical(token, 6)
    own_col = lax.bitwise_and(lax.shift_right_logical(token, 2), 3)
    place = lax.broadcasted_iota(jnp.int32, (1, 2 * AREA), 1)
    second = place >= AREA
    j = jnp.where(second, place - AREA, place)
    r_row = 2 - 3 * r
    side = jnp.where(j >= E_AT, j - E_AT, j - L_AT)
    side_row = jnp.where(side >= EDGE, r_row, lax.shift_right_arithmetic(side, 4))
    area_row = jnp.where(
        j >= L_AT, side_row, jnp.where(j >= R_AT, r_row, lax.shift_right_logical(j, 6))
    )
    area_col = jnp.where(
        j >= E_AT, 4,
        jnp.where(j >= L_AT, -1, lax.bitwise_and(lax.shift_right_logical(j, 2), 3)),
    )
    whole_col = area_col + 4 * c
    inside = (whole_col >= 0) & (whole_col < 4 * n_cols)
    dr = area_row - own_row
    dc = area_col - own_col
    near = (dr >= -1) & (dr <= 1) & (dc >= -1) & (dc <= 1) & inside
    code = jnp.where(near, 3 * dr + dc + 4, -1)
    later = jnp.minimum(p + 1, periods - 1)
    back_ok = link[p] * (p > 0).astype(jnp.int32)
    ahead_ok = link[later] * (p + 1 < periods).astype(jnp.int32)
    allow_f = jnp.zeros((OWN, 2 * AREA), jnp.int32)
    allow_b = jnp.zeros((OWN, 2 * AREA), jnp.int32)
    for o in range(9):
        own_ok = 1 if o == 4 else window[p, 1, o]
        at = code == o
        allow_f = jnp.where(at, jnp.where(second, window[p, 0, o] * back_ok, own_ok), allow_f)
        at = code == 8 - o
        allow_b = jnp.where(at, jnp.where(second, window[later, 0, o] * ahead_ok, own_ok), allow_b)
    bias_f[...] = jnp.where(allow_f > 0, 0.0, NEG)
    bias_b[...] = jnp.where(allow_b > 0, 0.0, NEG)

    hop(0)
    hop(1)
    after_t(0)
    after_r(0)
    after_t(1)
    after_tr(0)
    after_r(1)
    finish(0)

    lane = lax.broadcasted_iota(jnp.int32, (OWN, 128), 1)
    lane16 = lax.bitwise_and(lane, 15)

    def forward(h, acc):
        ch = pl.ds(pl.multiple_of(h * HD, HD), HD)
        vh = pl.ds(pl.multiple_of(channels + h * HD, HD), HD)
        scores = nt(qg[:OWN, ch], kv[:, ch]) * scale + bias_f[...]
        peak = jnp.max(scores, axis=1, keepdims=True)
        e = jnp.exp(scores - peak)
        total = jnp.sum(e, axis=1, keepdims=True)
        weights = e * (1.0 / total)
        out = nn(weights.astype(BF16), kv[:, vh]).astype(BF16)
        o_ref[:, ch] = out
        g = qg[:OWN, vh]
        delta = jnp.sum(g.astype(F32) * out.astype(F32), axis=1, keepdims=True)
        ds = (weights * (nt(g, kv[:, vh]) - delta)).astype(BF16)
        dq_ref[:, ch] = (nn(ds, kv[:, ch]) * scale).astype(BF16)
        acc = jnp.where(lane16 == h, peak + jnp.log(total), acc)
        return jnp.where(lane16 == h + heads, delta, acc)

    acc = jnp.zeros((OWN, 128), F32)
    if COMPUTE:
        acc = lax.fori_loop(0, heads, forward, acc, unroll=UNROLL)
    hi = acc.astype(BF16).astype(F32)
    mid = (acc - hi).astype(BF16).astype(F32)
    low = acc - hi - mid
    parts = jnp.where(lane < 16, hi, jnp.where(lane < 32, mid, low)).astype(BF16)
    sown[...] = parts
    stats[:OWN, :] = parts
    spack[...] = nn(edge_pick(ROWS), parts).astype(BF16)
    corner_at = pl.multiple_of(CORNER * (1 - r), CORNER)
    sops = []

    def stat(src, at, size, device):
        i = len(sops)
        op = copy(src, stats.at[pl.ds(at, size)], ssend, srecv, i, device)
        op.start()
        sops.append(op)

    for base, t in ((AREA, prv), (0, p)):
        stat(sown.at[pl.ds(half_at, HALF)], base + R_AT, HALF, (t, mate, c))
        stat(spack.at[pl.ds(corner_at, CORNER)], base + E_AT + EDGE, CORNER, (t, mate, left))
        stat(
            spack.at[pl.ds(pl.multiple_of(EDGE + corner_at, CORNER), CORNER)],
            base + L_AT + EDGE, CORNER, (t, mate, right),
        )
        stat(spack.at[pl.ds(0, EDGE)], base + E_AT, EDGE, (t, r, left))
        stat(spack.at[pl.ds(EDGE, EDGE)], base + L_AT, EDGE, (t, r, right))
        if base:
            stat(sown, base, OWN, (t, r, c))

    after_tr(1)
    finish(1)
    for op in sops:
        op.wait_recv()
    pick_row = lax.broadcasted_iota(jnp.int32, (16, 128), 0)
    pick_lane = lax.broadcasted_iota(jnp.int32, (16, 128), 1)
    pick = jnp.where((lax.bitwise_and(pick_lane, 15) == pick_row) & (pick_lane < 48), 1.0, 0.0)
    stat_rows[...] = nt(pick.astype(BF16), stats[...])

    def backward(h, carry):
        ch = pl.ds(pl.multiple_of(h * HD, HD), HD)
        vh = pl.ds(pl.multiple_of(channels + h * HD, HD), HD)
        scores = nt(kv[:OWN, ch], qg[:, ch]) * scale + bias_b[...]
        weights = jnp.exp(scores - stat_rows[pl.ds(h, 1), :])
        dv_ref[:, ch] = nn(weights.astype(BF16), qg[:, vh]).astype(BF16)
        dp = nt(kv[:OWN, vh], qg[:, vh])
        ds = (weights * (dp - stat_rows[pl.ds(h + heads, 1), :])).astype(BF16)
        dk_ref[:, ch] = (nn(ds, qg[:, ch]) * scale).astype(BF16)
        return carry

    if COMPUTE:
        lax.fori_loop(0, heads, backward, 0, unroll=UNROLL)
    for op in pending + sops:
        op.wait_send()


def body(query, key, value, out_grad, tile_window, period_link):
    channels = query.shape[-1]
    heads = channels // HD
    flat = [x.reshape(OWN, channels) for x in (query, key, value, out_grad)]
    whole = pl.BlockSpec(memory_space=pltpu.VMEM)
    table = pl.BlockSpec(memory_space=pltpu.SMEM)
    outs = pl.pallas_call(
        functools.partial(
            kernel, heads=heads, periods=lax.axis_size("tm"), n_cols=lax.axis_size("col")
        ),
        out_shape=[jax.ShapeDtypeStruct((OWN, channels), BF16)] * 4,
        in_specs=[table, table] + [whole] * 4,
        out_specs=[whole] * 4,
        scratch_shapes=[
            pltpu.VMEM((2 * AREA, 2 * channels), BF16),
            pltpu.VMEM((2 * AREA, 2 * channels), BF16),
            pltpu.VMEM((2 * AREA, 128), BF16),
            pltpu.VMEM((2, 2, HALF // 2, 2 * channels), BF16),
            pltpu.VMEM((2, 2 * EDGE, 2 * channels), BF16),
            pltpu.VMEM((2, 2 * CORNER, 2 * channels), BF16),
            pltpu.VMEM((2, 2 * EDGE, 2 * channels), BF16),
            pltpu.VMEM((2, 2 * CORNER, 2 * channels), BF16),
            pltpu.VMEM((2 * EDGE, 128), BF16),
            pltpu.VMEM((OWN, 128), BF16),
            pltpu.VMEM((OWN, 2 * AREA), F32),
            pltpu.VMEM((OWN, 2 * AREA), F32),
            pltpu.VMEM((2 * heads, 2 * AREA), F32),
            pltpu.SemaphoreType.DMA((22,)),
            pltpu.SemaphoreType.DMA((22,)),
            pltpu.SemaphoreType.DMA((8,)),
            pltpu.SemaphoreType.DMA((8,)),
            pltpu.SemaphoreType.DMA((11,)),
            pltpu.SemaphoreType.DMA((11,)),
        ],
        compiler_params=pltpu.CompilerParams(
            collective_id=0, has_side_effects=True, vmem_limit_bytes=48 * 1024 * 1024
        ),
    )(tile_window, period_link, *flat)
    return tuple(x.reshape(query.shape) for x in outs)


def solution(mesh):
    spread = P("tm", "row", "col", None)
    return jax.shard_map(
        body,
        mesh=mesh,
        in_specs=(spread, spread, spread, spread, P(), P()),
        out_specs=(spread, spread, spread, spread),
        check_vma=False,
    )
```

profile of v0, /device:TPU:1, one launch (start us, length us, event | category | flops | bytes accessed | tf_op | source)
XLA Modules:
  0.0 96.6 jit_solution(11080788714353066244)
XLA Ops:
  0.6 0.0 copy-start.4
  0.6 0.8 copy.10.window
  1.5 0.0 copy-done.4
  1.5 0.0 copy-start
  1.5 0.9 copy-done
  2.4 0.0 copy-start.1
  2.4 0.9 copy-done.1
  3.4 0.0 copy-start.2
  3.4 0.9 copy-done.2
  4.3 0.0 copy-start.3
  4.3 0.9 copy-done.3
  5.3 88.5 %shard_map.93 = (bf16[128,1024]{1,0:T(8,128)(2,1)S(1)}, bf16[128,1024]{1,0:T(8,128)(2,1)S(1)}, bf16[128,1024]{1,0:T(8,128)(2,1)S(1)}, bf16[128,1024]{1,0:T(8,128)(2,1)S(1)}) custom-call(s32[64,2,9]{2,1,0:T(2,128)S(1)} %copy.10.window, s32[64]{0:T(128)S(1)} %copy-done.4, bf16[128,1024]{1,0:T(8,128)(2,1)S(1)} %bitcast.12, bf16[128,1024]{1,0:T(8,128)(2,1)S(1)} %bitcast.13, ...), custom_call_target="tpu_custom_call" | custom-call | tf_op jit(solution)/shard_map/pallas_call | solution.py:306
  93.8 0.7 copy.15
  94.5 0.7 copy.16
  95.2 0.7 copy.17
  95.9 0.7 copy.18
Async XLA Ops:
  0.6 0.8 copy-start.4
  1.5 1.0 copy-start
  2.4 0.9 copy-start.1
  3.4 0.9 copy-start.2
  4.3 0.9 copy-start.3
where the time goes:
time: 96.9 us; the launch traced here: 96.6 us
  Pallas kernels  88.5 us (91%)
  local copies, waits for them, and re-layouts  7.42 us (8%)
    pallas_call x1, Pallas kernels, body(): pl.pallas_call(functools.partial(kernel, heads=heads, periods=lax.axis_si...  88.5 us
    unnamed x15, local copies, waits for them, and re-layouts  7.42 us

commit v1 on v0

v1 whole, which is shorter than its diff:
```python
import functools
import math

import jax
import jax.numpy as jnp
from jax import lax
from jax.experimental import pallas as pl
from jax.experimental.pallas import tpu as pltpu
from jax.sharding import PartitionSpec as P

HD = 128
S = 4
ROWS = 8
COLS = 16
OWN = ROWS * COLS
HALF = S * COLS
EDGE = ROWS * S
CORNER = S * S
SIDE = EDGE + CORNER
AREA = OWN + HALF + 2 * SIDE
R_AT = OWN
L_AT = OWN + HALF
E_AT = L_AT + SIDE
NEG = -1e30
MESH = pl.DeviceIdType.MESH
F32 = jnp.float32
BF16 = jnp.bfloat16

UNROLL = 8
MAIN = AREA + OWN
REST = 2 * AREA - MAIN
PLAN = (
    "load0", "R0", "T0", "E0", "load1", "mask", "sent0", "R1", "T1", "E1", "t0", "r0", "tr0",
    "near0", "far0", "F", "stat", "r1", "t1", "near1", "B1", "tr1", "far1", "B2",
)


def nt(a, b):
    return lax.dot_general(a, b, (((1,), (1,)), ((), ())), preferred_element_type=F32)


def nn(a, b):
    return lax.dot_general(a, b, (((1,), (0,)), ((), ())), preferred_element_type=F32)


def edge_pick(rows):
    count = rows * S
    out = lax.broadcasted_iota(jnp.int32, (2 * count, rows * COLS), 0)
    src = lax.broadcasted_iota(jnp.int32, (2 * count, rows * COLS), 1)
    right = (out >= count).astype(jnp.int32)
    place = out - right * count
    want = lax.shift_right_logical(place, 2) * COLS + lax.bitwise_and(place, 3) + right * (COLS - S)
    return jnp.where(src == want, 1.0, 0.0).astype(BF16)


def kernel(
    window, link, q_ref, k_ref, v_ref, g_ref, o_out, dq_out, dk_out, dv_out,
    kv, qg, stats, pack_own, pack_r, pack_t, pack_tr, spack, sown, bias_f, bias_b, bias_rest,
    stat_rows, o_ref, dq_ref, dk_ref, dv_ref, dk_sum, dv_sum,
    local, send, recv, ssend, srecv, *, heads, periods, n_cols,
):
    channels = heads * HD
    scale = 1.0 / math.sqrt(HD)
    p = lax.axis_index("tm")
    r = lax.axis_index("row")
    c = lax.axis_index("col")
    nxt = lax.rem(p + 1, periods)
    prv = lax.rem(p + periods - 1, periods)
    mate = 1 - r
    has_left = c > 0
    has_right = c < n_cols - 1
    left = jnp.maximum(c - 1, 0)
    right = jnp.minimum(c + 1, n_cols - 1)
    bufs = (kv, qg)
    toward = (nxt, prv)

    loads = []
    for i, (src, buf, at) in enumerate(
        ((k_ref, kv, 0), (v_ref, kv, channels), (q_ref, qg, 0), (g_ref, qg, channels))
    ):
        op = pltpu.make_async_copy(src, buf.at[pl.ds(0, OWN), pl.ds(at, channels)], local.at[i])
        op.start()
        loads.append(op)

    barrier = pltpu.get_barrier_semaphore()

    def greet(*friends):
        for friend in friends:
            pl.semaphore_signal(barrier, inc=1, device_id=friend, device_id_type=MESH)

    greet((p, mate, c), (nxt, r, c), (prv, r, c), (nxt, mate, c), (prv, mate, c))

    @pl.when(has_left)
    def _():
        greet(*[(t, row, left) for t in (p, nxt, prv) for row in (r, mate)])

    @pl.when(has_right)
    def _():
        greet(*[(t, row, right) for t in (p, nxt, prv) for row in (r, mate)])

    both = 5 + 6 * has_left.astype(jnp.int32) + 6 * has_right.astype(jnp.int32)
    pl.semaphore_wait(barrier, both)

    for missing, at in ((has_left, L_AT), (has_right, E_AT)):

        @pl.when(jnp.logical_not(missing))
        def _():
            for base in (0, AREA):
                for buf in (kv, qg):
                    buf[pl.ds(base + at, SIDE), :] = jnp.zeros((SIDE, 2 * channels), BF16)
                stats[pl.ds(base + at, SIDE), :] = jnp.zeros((SIDE, 128), BF16)

    half_at = pl.multiple_of(HALF * (1 - r), HALF)
    corner_at = pl.multiple_of(CORNER * (1 - r), CORNER)
    NAMES = ("R", "T", "TR", "le", "re", "lc", "rc", "tle", "tre", "tlc", "trc")
    pending, lefts, rights = [], [], []

    def copy(src, dst, a, b, i, device):
        return pltpu.make_async_remote_copy(
            src_ref=src, dst_ref=dst, send_sem=a.at[i], recv_sem=b.at[i],
            device_id=device, device_id_type=MESH,
        )

    got = {}

    def make(x, name, src, at, size, device):
        op = copy(src, bufs[x].at[pl.ds(at, size)], send, recv, x * 11 + NAMES.index(name), device)
        got[name, x] = op
        return op

    def go(*args):
        op = make(*args)
        op.start()
        pending.append(op)

    def sides(x, tag, pack, rows, base, shift):
        count = rows * S
        a = make(x, tag[0], pack.at[x, pl.ds(0, count)], base + E_AT + shift, count, (p, r, left))
        b = make(x, tag[1], pack.at[x, pl.ds(count, count)], base + L_AT + shift, count, (p, r, right))
        pl.when(has_left)(a.start)
        pl.when(has_right)(b.start)
        lefts.append(a)
        rights.append(b)

    def begin_r(x):
        go(x, "R", bufs[x].at[pl.ds(half_at, HALF)], R_AT, HALF, (p, mate, c))

    def begin_t(x):
        go(x, "T", bufs[x].at[pl.ds(0, OWN)], AREA, OWN, (toward[x], r, c))

    def begin_e(x):
        pack_own[x] = nn(edge_pick(ROWS), bufs[x][:OWN, :]).astype(BF16)
        sides(x, ("le", "re"), pack_own, ROWS, 0, 0)

    def after_r(x):
        got["R", x].wait_recv()
        turn = lax.rem(p, 8) == (7 if x == 0 else 0)
        at = pl.multiple_of(jnp.where(turn, half_at, R_AT), HALF)
        row = jnp.where(turn, mate, r)
        go(x, "TR", bufs[x].at[pl.ds(at, HALF)], AREA + R_AT, HALF, (toward[x], row, c))
        pack_r[x] = nn(edge_pick(S), bufs[x][R_AT:L_AT, :]).astype(BF16)
        sides(x, ("lc", "rc"), pack_r, S, 0, EDGE)

    def after_t(x):
        got["T", x].wait_recv()
        pack_t[x] = nn(edge_pick(ROWS), bufs[x][AREA:AREA + OWN, :]).astype(BF16)
        sides(x, ("tle", "tre"), pack_t, ROWS, AREA, 0)

    def after_tr(x):
        got["TR", x].wait_recv()
        pack_tr[x] = nn(edge_pick(S), bufs[x][AREA + R_AT:AREA + L_AT, :]).astype(BF16)
        sides(x, ("tlc", "trc"), pack_tr, S, AREA, EDGE)

    def arrived(x, from_right, from_left):
        @pl.when(has_right)
        def _():
            for name in from_right:
                got[name, x].wait_recv()

        @pl.when(has_left)
        def _():
            for name in from_left:
                got[name, x].wait_recv()

    def near(x):
        arrived(x, ("le", "lc"), ("re", "rc"))

    def far(x):
        arrived(x, ("tle", "tlc"), ("tre", "trc"))

    def codes(first, count):
        token = lax.broadcasted_iota(jnp.int32, (OWN, 1), 0)
        own_row = lax.shift_right_logical(token, 6)
        own_col = lax.bitwise_and(lax.shift_right_logical(token, 2), 3)
        place = lax.broadcasted_iota(jnp.int32, (1, count), 1) + first
        second = place >= AREA
        j = jnp.where(second, place - AREA, place)
        r_row = 2 - 3 * r
        side = jnp.where(j >= E_AT, j - E_AT, j - L_AT)
        side_row = jnp.where(side >= EDGE, r_row, lax.shift_right_arithmetic(side, 4))
        area_row = jnp.where(
            j >= L_AT, side_row, jnp.where(j >= R_AT, r_row, lax.shift_right_logical(j, 6))
        )
        area_col = jnp.where(
            j >= E_AT, 4,
            jnp.where(j >= L_AT, -1, lax.bitwise_and(lax.shift_right_logical(j, 2), 3)),
        )
        whole_col = area_col + 4 * c
        inside = (whole_col >= 0) & (whole_col < 4 * n_cols)
        dr = area_row - own_row
        dc = area_col - own_col
        close = (dr >= -1) & (dr <= 1) & (dc >= -1) & (dc <= 1) & inside
        return jnp.where(close, 3 * dr + dc + 4, -1), second

    def bias(first, count, source, ok, turned):
        code, second = codes(first, count)
        allow = jnp.zeros((OWN, count), jnp.int32)
        for o in range(9):
            own_ok = 1 if o == 4 else window[o, 1, p]
            entry = jnp.where(second, window[o, 0, source] * ok, own_ok)
            allow = jnp.where(code == (8 - o if turned else o), entry, allow)
        return jnp.where(allow > 0, 0.0, NEG)

    def masks():
        later = jnp.minimum(p + 1, periods - 1)
        back_ok = link[p] * (p > 0).astype(jnp.int32)
        ahead_ok = link[later] * (p + 1 < periods).astype(jnp.int32)
        bias_f[...] = bias(0, 2 * AREA, p, back_ok, False)
        bias_b[...] = bias(0, MAIN, later, ahead_ok, True)
        bias_rest[...] = bias(MAIN, REST, later, ahead_ok, True)

    lane = lax.broadcasted_iota(jnp.int32, (OWN, 128), 1)
    lane16 = lax.bitwise_and(lane, 15)

    def forward(h, total_stats):
        ch = pl.ds(pl.multiple_of(h * HD, HD), HD)
        vh = pl.ds(pl.multiple_of(channels + h * HD, HD), HD)
        scores = nt(qg[:OWN, ch], kv[:, ch]) * scale + bias_f[...]
        peak = jnp.max(scores, axis=1, keepdims=True)
        e = jnp.exp(scores - peak)
        total = jnp.sum(e, axis=1, keepdims=True)
        weights = e * (1.0 / total)
        out = nn(weights.astype(BF16), kv[:, vh]).astype(BF16)
        o_ref[:, ch] = out
        g = qg[:OWN, vh]
        delta = jnp.sum(g.astype(F32) * out.astype(F32), axis=1, keepdims=True)
        ds = (weights * (nt(g, kv[:, vh]) - delta)).astype(BF16)
        dq_ref[:, ch] = (nn(ds, kv[:, ch]) * scale).astype(BF16)
        total_stats = jnp.where(lane16 == h, peak + jnp.log(total), total_stats)
        return jnp.where(lane16 == h + heads, delta, total_stats)

    saves = []

    def save(pairs):
        for src, dst in pairs:
            op = pltpu.make_async_copy(src, dst, local.at[4 + len(saves)])
            op.start()
            saves.append(op)

    result = []

    def run_forward():
        zero = jnp.zeros((OWN, 128), F32)
        result.append(lax.fori_loop(0, heads, forward, zero, unroll=UNROLL))

    sops, slefts, srights = [], [], []

    def send_stats():
        value = result[0]
        hi = value.astype(BF16).astype(F32)
        mid = (value - hi).astype(BF16).astype(F32)
        low = value - hi - mid
        parts = jnp.where(lane < 16, hi, jnp.where(lane < 32, mid, low)).astype(BF16)
        sown[...] = parts
        stats[:OWN, :] = parts
        spack[...] = nn(edge_pick(ROWS), parts).astype(BF16)

        def stat(kept, src, at, size, device):
            i = len(sops) + len(slefts) + len(srights)
            op = copy(src, stats.at[pl.ds(at, size)], ssend, srecv, i, device)
            kept.append(op)

        right_corner = pl.multiple_of(EDGE + corner_at, CORNER)
        for base, t in ((0, p), (AREA, prv)):
            stat(sops, sown.at[pl.ds(half_at, HALF)], base + R_AT, HALF, (t, mate, c))
            stat(slefts, spack.at[pl.ds(corner_at, CORNER)], base + E_AT + EDGE, CORNER, (t, mate, left))
            stat(srights, spack.at[pl.ds(right_corner, CORNER)], base + L_AT + EDGE, CORNER, (t, mate, right))
            stat(slefts, spack.at[pl.ds(0, EDGE)], base + E_AT, EDGE, (t, r, left))
            stat(srights, spack.at[pl.ds(EDGE, EDGE)], base + L_AT, EDGE, (t, r, right))
        stat(sops, sown, AREA, OWN, (prv, r, c))
        for op in sops:
            op.start()

        @pl.when(has_left)
        def _():
            for op in slefts:
                op.start()

        @pl.when(has_right)
        def _():
            for op in srights:
                op.start()

        save(((o_ref, o_out), (dq_ref, dq_out)))

    def rows():
        for op in sops:
            op.wait_recv()

        @pl.when(has_right)
        def _():
            for op in slefts:
                op.wait_recv()

        @pl.when(has_left)
        def _():
            for op in srights:
                op.wait_recv()

        pick_row = lax.broadcasted_iota(jnp.int32, (16, 128), 0)
        pick_lane = lax.broadcasted_iota(jnp.int32, (16, 128), 1)
        same = lax.bitwise_and(pick_lane, 15) == pick_row
        pick = jnp.where(same & (pick_lane < 48), 1.0, 0.0)
        stat_rows[...] = nt(pick.astype(BF16), stats[:MAIN, :])
        return nt(pick.astype(BF16), stats[MAIN:, :])

    def backward(h, at, count, bias_now, lse, delta):
        ch = pl.ds(pl.multiple_of(h * HD, HD), HD)
        vh = pl.ds(pl.multiple_of(channels + h * HD, HD), HD)
        span = pl.ds(at, count)
        scores = nt(kv[:OWN, ch], qg[span, ch]) * scale + bias_now
        weights = jnp.exp(scores - lse)
        dv = nn(weights.astype(BF16), qg[span, vh])
        dp = nt(kv[:OWN, vh], qg[span, vh])
        ds = (weights * (dp - delta)).astype(BF16)
        return nn(ds, qg[span, ch]), dv

    kept = []

    def main_backward():
        kept.append(rows())

        def one(h, carry):
            ch = pl.ds(pl.multiple_of(h * HD, HD), HD)
            lse = stat_rows[pl.ds(h, 1), :]
            delta = stat_rows[pl.ds(h + heads, 1), :]
            dk, dv = backward(h, 0, MAIN, bias_b[...], lse, delta)
            dk_sum[:, ch] = dk
            dv_sum[:, ch] = dv
            return carry

        lax.fori_loop(0, heads, one, 0, unroll=UNROLL)

    def rest_backward():
        for h in range(heads):
            ch = pl.ds(h * HD, HD)
            lse = kept[0][h:h + 1, :]
            delta = kept[0][h + heads:h + heads + 1, :]
            dk, dv = backward(h, MAIN, REST, bias_rest[...], lse, delta)
            dk_ref[:, ch] = ((dk_sum[:, ch] + dk) * scale).astype(BF16)
            dv_ref[:, ch] = (dv_sum[:, ch] + dv).astype(BF16)
        save(((dk_ref, dk_out), (dv_ref, dv_out)))

    def load(x):
        loads[2 * x].wait()
        loads[2 * x + 1].wait()

    steps = {
        "R": begin_r, "T": begin_t, "E": begin_e, "r": after_r, "t": after_t, "tr": after_tr,
        "near": near, "far": far, "load": load, "sent": lambda x: got["R", x].wait_send(),
    }
    plain = {
        "mask": masks, "F": run_forward, "stat": send_stats, "B1": main_backward, "B2": rest_backward,
    }
    done_sends = []
    for word in PLAN:
        if word in plain:
            plain[word]()
        else:
            steps[word[:-1]](int(word[-1]))
            if word[:-1] == "sent":
                done_sends.append(got["R", int(word[-1])])
    for op in pending + sops:
        if not any(op is one for one in done_sends):
            op.wait_send()

    @pl.when(has_left)
    def _():
        for op in lefts + slefts:
            op.wait_send()

    @pl.when(has_right)
    def _():
        for op in rights + srights:
            op.wait_send()

    for op in saves:
        op.wait()


def flush(*refs):
    count = len(refs) // 2
    ops = [pltpu.make_async_copy(refs[i], refs[count + i], refs[-1].at[i]) for i in range(count)]
    for op in ops:
        op.start()
    for op in ops:
        op.wait()


def body(query, key, value, out_grad, tile_window, period_link):
    channels = query.shape[-1]
    heads = channels // HD
    flat = [x.reshape(OWN, channels) for x in (query, key, value, out_grad)]
    whole = pl.BlockSpec(memory_space=pltpu.HBM)
    shapes = [jax.ShapeDtypeStruct((OWN, channels), BF16)] * 4
    table = pl.BlockSpec(memory_space=pltpu.SMEM)
    outs = pl.pallas_call(
        functools.partial(
            kernel, heads=heads, periods=lax.axis_size("tm"), n_cols=lax.axis_size("col")
        ),
        out_shape=shapes,
        in_specs=[table, table] + [whole] * 4,
        out_specs=[whole] * 4,
        scratch_shapes=[
            pltpu.VMEM((2 * AREA, 2 * channels), BF16),
            pltpu.VMEM((2 * AREA, 2 * channels), BF16),
            pltpu.VMEM((2 * AREA, 128), BF16),
            pltpu.VMEM((2, 2 * EDGE, 2 * channels), BF16),
            pltpu.VMEM((2, 2 * CORNER, 2 * channels), BF16),
            pltpu.VMEM((2, 2 * EDGE, 2 * channels), BF16),
            pltpu.VMEM((2, 2 * CORNER, 2 * channels), BF16),
            pltpu.VMEM((2 * EDGE, 128), BF16),
            pltpu.VMEM((OWN, 128), BF16),
            pltpu.VMEM((OWN, 2 * AREA), F32),
            pltpu.VMEM((OWN, MAIN), F32),
            pltpu.VMEM((OWN, REST), F32),
            pltpu.VMEM((2 * heads, MAIN), F32),
            pltpu.VMEM((OWN, channels), BF16),
            pltpu.VMEM((OWN, channels), BF16),
            pltpu.VMEM((OWN, channels), BF16),
            pltpu.VMEM((OWN, channels), BF16),
            pltpu.VMEM((OWN, channels), F32),
            pltpu.VMEM((OWN, channels), F32),
            pltpu.SemaphoreType.DMA((8,)),
            pltpu.SemaphoreType.DMA((22,)),
            pltpu.SemaphoreType.DMA((22,)),
            pltpu.SemaphoreType.DMA((11,)),
            pltpu.SemaphoreType.DMA((11,)),
        ],
        compiler_params=pltpu.CompilerParams(
            collective_id=0, has_side_effects=True, vmem_limit_bytes=63 * 1024 * 1024
        ),
    )(tile_window.transpose(2, 1, 0), period_link, *flat)
    outs = pl.pallas_call(
        flush,
        out_shape=shapes,
        in_specs=[whole] * 4,
        out_specs=[whole] * 4,
        scratch_shapes=[pltpu.SemaphoreType.DMA((4,))],
        compiler_params=pltpu.CompilerParams(vmem_limit_bytes=63 * 1024 * 1024),
    )(*outs)
    return tuple(x.reshape(query.shape) for x in outs)


def solution(mesh):
    spread = P("tm", "row", "col", None)
    return jax.shard_map(
        body,
        mesh=mesh,
        in_specs=(spread, spread, spread, spread, P(), P()),
        out_specs=(spread, spread, spread, spread),
        check_vma=False,
    )
```

time: 96.9 us -> 115 us (1.19)
  the two profiles are of different devices: /device:TPU:1 before, /device:TPU:48 now
where the time goes in v1:
time: 115 us
  Pallas kernels  114 us (99%)
    pallas_call x1, Pallas kernels, body(): pl.pallas_call(functools.partial(kernel, heads=heads, periods=lax.axis_si...  81.1 us
    pallas_call x1, Pallas kernels, body(): pl.pallas_call(flush, out_shape=shapes, in_specs=[whole] * 4, out_specs=[...  32.9 us

profile of v1, /device:TPU:48, one launch (start us, length us, event | category | flops | bytes accessed | tf_op | source)
XLA Modules:
  0.0 114.6 jit_solution(13003675215750177483)
XLA Ops:
  0.6 81.1 %shard_map.93 = (bf16[128,1024]{1,0:T(8,128)(2,1)}, bf16[128,1024]{1,0:T(8,128)(2,1)}, bf16[128,1024]{1,0:T(8,128)(2,1)}, bf16[128,1024]{1,0:T(8,128)(2,1)}) custom-call(s32[9,2,64]{2,1,0:T(2,128)} %bitcast.13, s32[64]{0:T(128)} %link.1, bf16[128,1024]{1,0:T(8,128)(2,1)} %bitcast.9, bf16[128,1024]{1,0:T(8,128)(2,1)} %bitcast.10, bf16[128,1024]{1,0:T(8,128)(2,1)} %bitcast.11, ...), custom_call_target="tpu_custom_call" | custom-call | tf_op jit(solution)/shard_map/pallas_call | solution.py:417
  81.7 32.9 %shard_map.94 = (bf16[128,1024]{1,0:T(8,128)(2,1)}, bf16[128,1024]{1,0:T(8,128)(2,1)}, bf16[128,1024]{1,0:T(8,128)(2,1)}, bf16[128,1024]{1,0:T(8,128)(2,1)}) custom-call(bf16[128,1024]{1,0:T(8,128)(2,1)} %get-tuple-element.12.refs_0_, bf16[128,1024]{1,0:T(8,128)(2,1)} %get-tuple-element.13.refs_1_, bf16[128,1024]{1,0:T(8,128)(2,1)} %get-tuple-element.14.refs_2_, ...), custom_call_target="tpu_custom_call" | custom-call | tf_op jit(solution)/shard_map/pallas_call | solution.py:454

commit v2 on v1

--- a/solution.py
+++ b/solution.py
@@ -30,8 +30,8 @@
 MAIN = AREA + OWN
 REST = 2 * AREA - MAIN
 PLAN = (
-    "load0", "R0", "T0", "E0", "load1", "mask", "sent0", "R1", "T1", "E1", "t0", "r0", "tr0",
-    "near0", "far0", "F", "stat", "r1", "t1", "near1", "B1", "tr1", "far1", "B2",
+    "load0", "R0", "T0", "E0", "load1", "mask", "E1", "r0", "t0", "R1", "tr0", "T1", "near0",
+    "far0", "F", "stat", "r1", "t1", "near1", "B1", "tr1", "far1", "B2",
 )
 
 
@@ -399,11 +399,16 @@
 
 
 def flush(*refs):
-    count = len(refs) // 2
-    ops = [pltpu.make_async_copy(refs[i], refs[count + i], refs[-1].at[i]) for i in range(count)]
-    for op in ops:
+    count = (len(refs) - 2) // 3
+    sources, targets, held = refs[:count], refs[count:2 * count], refs[2 * count:3 * count]
+    loads = [pltpu.make_async_copy(sources[i], held[i], refs[-2].at[i]) for i in range(count)]
+    stores = [pltpu.make_async_copy(held[i], targets[i], refs[-1].at[i]) for i in range(count)]
+    for op in loads:
         op.start()
-    for op in ops:
+    for load, store in zip(loads, stores):
+        load.wait()
+        store.start()
+    for op in stores:
         op.wait()
 
 
@@ -456,7 +461,7 @@
         out_shape=shapes,
         in_specs=[whole] * 4,
         out_specs=[whole] * 4,
-        scratch_shapes=[pltpu.SemaphoreType.DMA((4,))],
+        scratch_shapes=[pltpu.VMEM((OWN, channels), BF16)] * 4 + [pltpu.SemaphoreType.DMA((4,))] * 2,
         compiler_params=pltpu.CompilerParams(vmem_limit_bytes=63 * 1024 * 1024),
     )(*outs)
     return tuple(x.reshape(query.shape) for x in outs)

time: 115 us -> 74.1 us (0.64)
  the two profiles are of different devices: /device:TPU:48 before, /device:TPU:142 now
where the time goes in v2:
time: 74.1 us; the launch traced here: 73.9 us
  Pallas kernels  73.2 us (99%)
    pallas_call x1, Pallas kernels, body(): pl.pallas_call(functools.partial(kernel, heads=heads, periods=lax.axis_si...  71.3 us
    pallas_call x1, Pallas kernels, body(): pl.pallas_call(flush, out_shape=shapes, in_specs=[whole] * 4, out_specs=[...  1.98 us

profile of v2, /device:TPU:142, one launch (start us, length us, event | category | flops | bytes accessed | tf_op | source)
XLA Modules:
  0.0 73.9 jit_solution(5159636068685769828)
XLA Ops:
  0.6 71.3 %shard_map.93 = (bf16[128,1024]{1,0:T(8,128)(2,1)}, bf16[128,1024]{1,0:T(8,128)(2,1)}, bf16[128,1024]{1,0:T(8,128)(2,1)}, bf16[128,1024]{1,0:T(8,128)(2,1)}) custom-call(s32[9,2,64]{2,1,0:T(2,128)} %bitcast.13, s32[64]{0:T(128)} %link.1, bf16[128,1024]{1,0:T(8,128)(2,1)} %bitcast.9, bf16[128,1024]{1,0:T(8,128)(2,1)} %bitcast.10, bf16[128,1024]{1,0:T(8,128)(2,1)} %bitcast.11, ...), custom_call_target="tpu_custom_call" | custom-call | tf_op jit(solution)/shard_map/pallas_call | solution.py:422
  71.9 2.0 %shard_map.94 = (bf16[128,1024]{1,0:T(8,128)(2,1)}, bf16[128,1024]{1,0:T(8,128)(2,1)}, bf16[128,1024]{1,0:T(8,128)(2,1)}, bf16[128,1024]{1,0:T(8,128)(2,1)}) custom-call(bf16[128,1024]{1,0:T(8,128)(2,1)} %get-tuple-element.12.refs_0_, bf16[128,1024]{1,0:T(8,128)(2,1)} %get-tuple-element.13.refs_1_, bf16[128,1024]{1,0:T(8,128)(2,1)} %get-tuple-element.14.refs_2_, ...), custom_call_target="tpu_custom_call" | custom-call | tf_op jit(solution)/shard_map/pallas_call | solution.py:459

commit v3 on v2

--- a/solution.py
+++ b/solution.py
@@ -30,8 +30,8 @@
 MAIN = AREA + OWN
 REST = 2 * AREA - MAIN
 PLAN = (
-    "load0", "R0", "T0", "E0", "load1", "mask", "E1", "r0", "t0", "R1", "tr0", "T1", "near0",
-    "far0", "F", "stat", "r1", "t1", "near1", "B1", "tr1", "far1", "B2",
+    "load0", "R0", "T0", "E0", "load1", "mask", "E1", "r0", "t0", "R1", "near0", "F1", "tr0",
+    "T1", "far0", "F", "stat", "r1", "t1", "near1", "B1", "tr1", "far1", "B2",
 )
 
 
@@ -55,8 +55,8 @@
 
 def kernel(
     window, link, q_ref, k_ref, v_ref, g_ref, o_out, dq_out, dk_out, dv_out,
-    kv, qg, stats, pack_own, pack_r, pack_t, pack_tr, spack, sown, bias_f, bias_b, bias_rest,
-    stat_rows, o_ref, dq_ref, dk_ref, dv_ref, dk_sum, dv_sum,
+    kv, qg, stats, pack_own, pack_r, pack_t, pack_tr, spack, sown, bias_f, bias_f2, bias_b, bias_rest,
+    stat_rows, o_ref, dq_ref, dk_ref, dv_ref, dk_sum, dv_sum, early_s, early_g,
     local, send, recv, ssend, srecv, *, heads, periods, n_cols,
 ):
     channels = heads * HD
@@ -225,27 +225,45 @@
         later = jnp.minimum(p + 1, periods - 1)
         back_ok = link[p] * (p > 0).astype(jnp.int32)
         ahead_ok = link[later] * (p + 1 < periods).astype(jnp.int32)
-        bias_f[...] = bias(0, 2 * AREA, p, back_ok, False)
+        bias_f[...] = bias(0, MAIN, p, back_ok, False)
+        bias_f2[...] = bias(MAIN, REST, p, back_ok, False)
         bias_b[...] = bias(0, MAIN, later, ahead_ok, True)
         bias_rest[...] = bias(MAIN, REST, later, ahead_ok, True)
 
     lane = lax.broadcasted_iota(jnp.int32, (OWN, 128), 1)
     lane16 = lax.bitwise_and(lane, 15)
+
+    def early_forward():
+        def one(h, carry):
+            ch = pl.ds(pl.multiple_of(h * HD, HD), HD)
+            vh = pl.ds(pl.multiple_of(channels + h * HD, HD), HD)
+            early_s[h] = nt(qg[:OWN, ch], kv[:MAIN, ch]) * scale + bias_f[...]
+            early_g[h] = nt(qg[:OWN, vh], kv[:MAIN, vh])
+            return carry
+
+        lax.fori_loop(0, heads, one, 0, unroll=UNROLL)
 
     def forward(h, total_stats):
         ch = pl.ds(pl.multiple_of(h * HD, HD), HD)
         vh = pl.ds(pl.multiple_of(channels + h * HD, HD), HD)
-        scores = nt(qg[:OWN, ch], kv[:, ch]) * scale + bias_f[...]
-        peak = jnp.max(scores, axis=1, keepdims=True)
-        e = jnp.exp(scores - peak)
-        total = jnp.sum(e, axis=1, keepdims=True)
-        weights = e * (1.0 / total)
-        out = nn(weights.astype(BF16), kv[:, vh]).astype(BF16)
+        s1 = early_s[h]
+        s2 = nt(qg[:OWN, ch], kv[MAIN:, ch]) * scale + bias_f2[...]
+        peak = jnp.maximum(jnp.max(s1, axis=1, keepdims=True), jnp.max(s2, axis=1, keepdims=True))
+        e1 = jnp.exp(s1 - peak)
+        e2 = jnp.exp(s2 - peak)
+        total = jnp.sum(e1, axis=1, keepdims=True) + jnp.sum(e2, axis=1, keepdims=True)
+        inverse = 1.0 / total
+        w1 = e1 * inverse
+        w2 = e2 * inverse
+        out = nn(w1.astype(BF16), kv[:MAIN, vh]) + nn(w2.astype(BF16), kv[MAIN:, vh])
+        out = out.astype(BF16)
         o_ref[:, ch] = out
         g = qg[:OWN, vh]
         delta = jnp.sum(g.astype(F32) * out.astype(F32), axis=1, keepdims=True)
-        ds = (weights * (nt(g, kv[:, vh]) - delta)).astype(BF16)
-        dq_ref[:, ch] = (nn(ds, kv[:, ch]) * scale).astype(BF16)
+        d1 = (w1 * (early_g[h] - delta)).astype(BF16)
+        d2 = (w2 * (nt(g, kv[MAIN:, vh]) - delta)).astype(BF16)
+        dq = nn(d1, kv[:MAIN, ch]) + nn(d2, kv[MAIN:, ch])
+        dq_ref[:, ch] = (dq * scale).astype(BF16)
         total_stats = jnp.where(lane16 == h, peak + jnp.log(total), total_stats)
         return jnp.where(lane16 == h + heads, delta, total_stats)
 
@@ -370,7 +388,7 @@
         "near": near, "far": far, "load": load, "sent": lambda x: got["R", x].wait_send(),
     }
     plain = {
-        "mask": masks, "F": run_forward, "stat": send_stats, "B1": main_backward, "B2": rest_backward,
+        "mask": masks, "F1": early_forward, "F": run_forward, "stat": send_stats, "B1": main_backward, "B2": rest_backward,
     }
     done_sends = []
     for word in PLAN:
@@ -436,7 +454,8 @@
             pltpu.VMEM((2, 2 * CORNER, 2 * channels), BF16),
             pltpu.VMEM((2 * EDGE, 128), BF16),
             pltpu.VMEM((OWN, 128), BF16),
-            pltpu.VMEM((OWN, 2 * AREA), F32),
+            pltpu.VMEM((OWN, MAIN), F32),
+            pltpu.VMEM((OWN, REST), F32),
             pltpu.VMEM((OWN, MAIN), F32),
             pltpu.VMEM((OWN, REST), F32),
             pltpu.VMEM((2 * heads, MAIN), F32),
@@ -446,6 +465,8 @@
             pltpu.VMEM((OWN, channels), BF16),
             pltpu.VMEM((OWN, channels), F32),
             pltpu.VMEM((OWN, channels), F32),
+            pltpu.VMEM((heads, OWN, MAIN), F32),
+            pltpu.VMEM((heads, OWN, MAIN), F32),
             pltpu.SemaphoreType.DMA((8,)),
             pltpu.SemaphoreType.DMA((22,)),
             pltpu.SemaphoreType.DMA((22,)),

time: 74.1 us -> 74.2 us (level)
  no operation moved by 1% of the time
where the time goes in v3:
time: 74.2 us; the launch traced here: 74 us
  Pallas kernels  73.3 us (99%)
    pallas_call x1, Pallas kernels, body(): pl.pallas_call(functools.partial(kernel, heads=heads, periods=lax.axis_si...  71.3 us
    pallas_call x1, Pallas kernels, body(): pl.pallas_call(flush, out_shape=shapes, in_specs=[whole] * 4, out_specs=[...  1.98 us

profile of v3, /device:TPU:142, one launch (start us, length us, event | category | flops | bytes accessed | tf_op | source)
XLA Modules:
  0.0 74.0 jit_solution(6887527821074003719)
XLA Ops:
  0.6 71.3 %shard_map.93 = (bf16[128,1024]{1,0:T(8,128)(2,1)}, bf16[128,1024]{1,0:T(8,128)(2,1)}, bf16[128,1024]{1,0:T(8,128)(2,1)}, bf16[128,1024]{1,0:T(8,128)(2,1)}) custom-call(s32[9,2,64]{2,1,0:T(2,128)} %bitcast.13, s32[64]{0:T(128)} %link.1, bf16[128,1024]{1,0:T(8,128)(2,1)} %bitcast.9, bf16[128,1024]{1,0:T(8,128)(2,1)} %bitcast.10, bf16[128,1024]{1,0:T(8,128)(2,1)} %bitcast.11, ...), custom_call_target="tpu_custom_call" | custom-call | tf_op jit(solution)/shard_map/pallas_call | solution.py:440
  72.0 2.0 %shard_map.94 = (bf16[128,1024]{1,0:T(8,128)(2,1)}, bf16[128,1024]{1,0:T(8,128)(2,1)}, bf16[128,1024]{1,0:T(8,128)(2,1)}, bf16[128,1024]{1,0:T(8,128)(2,1)}) custom-call(bf16[128,1024]{1,0:T(8,128)(2,1)} %get-tuple-element.12.refs_0_, bf16[128,1024]{1,0:T(8,128)(2,1)} %get-tuple-element.13.refs_1_, bf16[128,1024]{1,0:T(8,128)(2,1)} %get-tuple-element.14.refs_2_, ...), custom_call_target="tpu_custom_call" | custom-call | tf_op jit(solution)/shard_map/pallas_call | solution.py:480

commit v4 on v2

--- a/solution.py
+++ b/solution.py
@@ -359,7 +359,9 @@
             dk, dv = backward(h, MAIN, REST, bias_rest[...], lse, delta)
             dk_ref[:, ch] = ((dk_sum[:, ch] + dk) * scale).astype(BF16)
             dv_ref[:, ch] = (dv_sum[:, ch] + dv).astype(BF16)
-        save(((dk_ref, dk_out), (dv_ref, dv_out)))
+            if h % 4 == 3:
+                half = (pl.ds(0, OWN), pl.ds((h - 3) * HD, 4 * HD))
+                save(((dk_ref.at[half], dk_out.at[half]), (dv_ref.at[half], dv_out.at[half])))
 
     def load(x):
         loads[2 * x].wait()
@@ -446,7 +448,7 @@
             pltpu.VMEM((OWN, channels), BF16),
             pltpu.VMEM((OWN, channels), F32),
             pltpu.VMEM((OWN, channels), F32),
-            pltpu.SemaphoreType.DMA((8,)),
+            pltpu.SemaphoreType.DMA((10,)),
             pltpu.SemaphoreType.DMA((22,)),
             pltpu.SemaphoreType.DMA((22,)),
             pltpu.SemaphoreType.DMA((11,)),

time: 74.1 us -> 74.1 us (level)
  no operation moved by 1% of the time
where the time goes in v4:
time: 74.1 us; the launch traced here: 73.8 us
  Pallas kernels  73.2 us (99%)
    pallas_call x1, Pallas kernels, body(): pl.pallas_call(functools.partial(kernel, heads=heads, periods=lax.axis_si...  71.2 us
    pallas_call x1, Pallas kernels, body(): pl.pallas_call(flush, out_shape=shapes, in_specs=[whole] * 4, out_specs=[...  1.98 us

profile of v4, /device:TPU:142, one launch (start us, length us, event | category | flops | bytes accessed | tf_op | source)
XLA Modules:
  0.0 73.8 jit_solution(8708519084862564841)
XLA Ops:
  0.6 71.2 %shard_map.93 = (bf16[128,1024]{1,0:T(8,128)(2,1)}, bf16[128,1024]{1,0:T(8,128)(2,1)}, bf16[128,1024]{1,0:T(8,128)(2,1)}, bf16[128,1024]{1,0:T(8,128)(2,1)}) custom-call(s32[9,2,64]{2,1,0:T(2,128)} %bitcast.13, s32[64]{0:T(128)} %link.1, bf16[128,1024]{1,0:T(8,128)(2,1)} %bitcast.9, bf16[128,1024]{1,0:T(8,128)(2,1)} %bitcast.10, bf16[128,1024]{1,0:T(8,128)(2,1)} %bitcast.11, ...), custom_call_target="tpu_custom_call" | custom-call | tf_op jit(solution)/shard_map/pallas_call | solution.py:424
  71.8 2.0 %shard_map.94 = (bf16[128,1024]{1,0:T(8,128)(2,1)}, bf16[128,1024]{1,0:T(8,128)(2,1)}, bf16[128,1024]{1,0:T(8,128)(2,1)}, bf16[128,1024]{1,0:T(8,128)(2,1)}) custom-call(bf16[128,1024]{1,0:T(8,128)(2,1)} %get-tuple-element.12.refs_0_, bf16[128,1024]{1,0:T(8,128)(2,1)} %get-tuple-element.13.refs_1_, bf16[128,1024]{1,0:T(8,128)(2,1)} %get-tuple-element.14.refs_2_, ...), custom_call_target="tpu_custom_call" | custom-call | tf_op jit(solution)/shard_map/pallas_call | solution.py:461
